TPU v7x, 32 devices: a whole 2x2x4 slice. The times are simulated.
32 devices in a mesh: seg: 2 (over x), smp: 8 (over z, y), snp: 2 (over core).
Axes of the slice: x: 2, y: 2, z: 4, core: 2. Of those that a mesh axis runs over, the one named last changes fastest.
Arguments:
- dosage: bfloat16 [4096, 8192], P('smp', ('seg', 'snp')), parts along dimension 1, may hold values from -48 to 48, as said below
Outputs:
- band_corr: float32 [3, 16, 512, 512], P(None, ('seg', 'snp'), 'smp'), parts along dimension 1
There are 2 independent parts, one for each index of `seg`. A program takes and returns all parts, laid end to end along the dimension named above; each array names one. Nothing has to cross between parts.
Inputs may be any that keep to these rules, and one draw needn't show every extreme that they name: `dosage`: dosages of each SNP share part of their variation with SNPs nearby.
All inputs are finite; a program needn't handle non-finite values.
Results may differ from a plain program's by a relative error of at most 0.0003.
Values may be sent and summed in bfloat16 or wider, within the bound.
A program may use at most 128 MiB of HBM per device.

v0:
```python
import jax
import jax.numpy as jnp
from jax import lax
from jax.sharding import PartitionSpec as P

BLK = 512


epsilon = 1e-06


def from_behind(x, axis, by):
    length = lax.axis_size(axis)
    pairs = [(i, i + by) for i in range(length) if 0 <= i + by < length]
    return lax.ppermute(x, axis, pairs)


def shards(dosage):
    sample_count = dosage.shape[0]
    block_count = dosage.shape[1] // BLK
    next_cols = from_behind(dosage[:, : 2 * BLK], "snp", -1)
    extended = jnp.concatenate([dosage, next_cols], axis=1)
    own_cube = dosage.reshape(sample_count, block_count, BLK)
    ext_cube = extended.reshape(sample_count, block_count + 2, BLK)

    def make_tiles(right_cube, offsets):
        tile_list = [
            jnp.einsum(
                "hmn,hmq->nmq",
                own_cube,
                right_cube[:, offset : offset + block_count],
                preferred_element_type=jnp.float32,
            )
            for offset in offsets
        ]
        return jnp.stack(tile_list, axis=1)

    tile_rows = BLK // lax.axis_size("smp")
    owned_zero = lax.psum_scatter(
        make_tiles(own_cube, (0,)), "smp", scatter_dimension=0, tiled=True
    )
    owned_band = lax.psum_scatter(
        make_tiles(ext_cube, (1, 2)), "smp", scatter_dimension=0, tiled=True
    )
    owned = jnp.concatenate([owned_zero, owned_band], axis=1)
    gram_tiles = jnp.transpose(owned, (1, 2, 0, 3))
    first_row = lax.axis_index("smp") * tile_rows
    squares = jnp.sum(jnp.square(extended.astype(jnp.float32)), axis=0)
    square_sums = lax.psum(squares, "smp").reshape(block_count + 2, BLK)
    row_sums = lax.dynamic_slice_in_dim(square_sums[:block_count], first_row, tile_rows, 1)
    row_scale = lax.rsqrt(row_sums + epsilon)
    col_scale = lax.rsqrt(square_sums + epsilon)
    col_stack = jnp.stack([col_scale[offset : offset + block_count] for offset in range(3)])
    return gram_tiles * row_scale[None, :, :, None] * col_stack[:, :, None, :]


def solution(mesh):
    return jax.shard_map(
        shards,
        mesh=mesh,
        in_specs=(P("smp", ("seg", "snp")),),
        out_specs=P(None, ("seg", "snp"), "smp", None),
        check_vma=False,
    )
```

profile of v0, /device:TPU:0, one launch (start us, length us, event | category | flops | bytes accessed | tf_op | source)
XLA Modules:
  0.0 461.5 jit_solution(16435303125887998806)
XLA Ops:
  6.5 0.0 all-reduce.5.cloned.1.call-start
  6.5 2.3 slice.35
  8.8 1.3 collective-permute-start
  10.1 5.5 %convolution_bitcast_fusion.2 = f32[512,1,4,512]{0,3,2,1:T(8,128)} fusion(bf16[64,4,8,512]{3,2,1,0:T(8,128)(2,1)} %bitcast.30), kind=kOutput, calls=%fused_computation.4 | convolution fusion | flops 1073741824 | bytes 6291456 | tf_op jit(solution)/shard_map/hmn,hmq->nmq/dot_general | solution.py:28
  15.5 5.4 %copy.18 = f32[512,1,4,512]{3,2,1,0:T(4,128)} copy(f32[512,1,4,512]{0,3,2,1:T(8,128)} %convolution_bitcast_fusion.2) | data formatting | bytes 8388608 | tf_op jit(solution)/shard_map/stack | solution.py:36
  21.0 1.8 constant_dynamic-update-slice_fusion.1
  22.8 0.0 collective-permute-done
  22.8 1.3 constant_dynamic-update-slice_fusion
  24.1 2.8 copy.19
  26.9 0.0 copy-start
  26.9 0.0 copy-start.1
  26.9 3.6 convolution_bitcast_fusion
  30.5 0.0 copy-done
  30.5 0.1 copy-done.1
  30.7 1.3 convolution_bitcast_fusion.1
  31.9 4.3 pad_maximum_fusion
  36.2 10.3 %copy.22 = f32[512,2,4,512]{3,2,1,0:T(4,128)} copy(f32[512,2,4,512]{0,3,2,1:T(8,128)} %pad_maximum_fusion) | data formatting | bytes 16777216 | tf_op jit(solution)/shard_map/stack | solution.py:36
  46.5 0.0 copy-start.2
  46.5 0.0 all-reduce.5.cloned.1.call-update
  46.5 0.6 copy-done.2
  47.1 0.6 dynamic-slice
  48.4 0.7 multiply_reduce_fusion
  49.0 41.0 %psum.7 = f32[3072]{0:T(1024)S(1)} all-reduce(f32[3072]{0:T(1024)S(1)} %multiply_reduce_fusion), channel_id=1, replica_groups=mesh['seg'=2,'smp'=8,'snp'=2] {'smp'}, use_global_device_ids=true, to_apply=%region_3.0 | all-reduce | flops 3072 | bytes 24576 | tf_op jit(solution)/shard_map/psum | solution.py:49
  90.1 0.1 add_rsqrt_fusion.1
  90.2 0.1 copy.23
  90.3 360.0 %all-reduce.5.cloned.1.call-done = (f32[512,2,4,512]{3,2,1,0:T(4,128)}, f32[512,1,4,512]{3,2,1,0:T(4,128)}) async-done(((f32[512,2,4,512]{3,2,1,0:T(4,128)}, f32[512,1,4,512]{3,2,1,0:T(4,128)}), (f32[512,2,4,512]{3,2,1,0:T(4,128)}, f32[512,1,4,512]{3,2,1,0:T(4,128)})) %all-reduce.5.cloned.1.call-update) | async-done | bytes 12582928
  450.3 1.3 constant_dynamic-slice_fusion
  451.6 1.1 constant_dynamic-slice_fusion.1
  452.7 0.4 fusion.7
  453.1 1.6 copy.24
  (8 shorter events, 0.1 us)
Async XLA Ops:
  6.5 443.7 %all-reduce.5.cloned.1.call-start = ((), (), s32[]{:S(2)}) async-start(), calls=%async_computation | async-start | bytes 25165824
  8.8 14.0 %collective-permute-start = (bf16[512,1024]{1,0:T(8,128)(2,1)}, bf16[512,1024]{1,0:T(8,128)(2,1)}, u32[]{:S(2)}, u32[]{:S(2)}) collective-permute-start(bf16[512,1024]{1,0:T(8,128)(2,1)} %slice.35), channel_id=1, source_target_pairs={{1,0},{3,2},{5,4},{7,6},{9,8},{11,10},{13,12},{15,14},{17,16},{19,... | collective-permute-start | bytes 3145736 | tf_op jit(solution)/shard_map/ppermute | solution.py:15
  26.9 3.6 copy-start
  26.9 3.8 copy-start.1
  46.5 0.7 copy-start.2
Sparse Core Ops, SparseCore 0:
  46.6 403.5 all-reduce.4
where the time goes:
time: 462 us
  waiting for transfers between devices  360 us (78%)
  blocking collectives  41 us (9%)
  local copies, waits for them, and re-layouts  29.3 us (6%)
  between operations  14.1 us (3%)
  matrix products  10.3 us (2%)
  other arithmetic  5.45 us (1%)
    unnamed x2, waiting for transfers between devices  360 us
    psum x1, blocking collectives, shards(): square_sums = lax.psum(squares, 'smp').reshape(block_count + 2, BLK)  41 us
    another operation x2, local copies, waits for them, and re-layouts, make_tiles(): return jnp.stack(tile_list, axis=1)  15.7 us
    dot_general x3, matrix products, make_tiles(): jnp.einsum('hmn,hmq->nmq', own_cube, right_cube[:, offset:offset + block_...  10.3 us
  transfers between devices with their start and end apart: 2, of which 1 were waited for; matrix products, arithmetic and copies ran while one was open for 3% of the time, Pallas kernels for 0%

commit v1 on v0

v1 whole, which is shorter than its diff:
```python
import functools

import jax
import jax.numpy as jnp
from jax import lax
from jax.experimental import pallas as pl
from jax.experimental.pallas import tpu as pltpu
from jax.sharding import PartitionSpec as P

BLK = 512
EPS = 1e-06
WIRE = jnp.float32
UNIT = 1.0
LAG = 3


def kernel(n, snps, x_ref, out_ref, full, squares_all, scale, row_scale, acc, level_send, level_recv,
           far_send, far_recv, next_squares, local_sem, raw_ss, raw_rs, core_ss, core_rs, fwd_ss, fwd_rs,
           sq_ss, sq_rs, nsq_ss, nsq_rs, lev_ss, lev_rs, far_ss, far_rs):
    samples, cols = x_ref.shape
    blocks = cols // BLK
    quarter = BLK // 4
    me = lax.axis_index("smp")
    core = lax.axis_index("snp")
    has_next = core < snps - 1
    has_prev = core > 0
    near_bit, far_bit = n // 4, n // 2
    near = (me // near_bit) % 2
    far = me // far_bit
    near_peer = me + near_bit * (1 - 2 * near)
    far_peer = me + far_bit * (1 - 2 * far)
    bits = []
    bit = n // 8
    while bit >= 1:
        bits.append(bit)
        bit //= 2
    tiles = 3 * blocks

    barrier = pltpu.get_barrier_semaphore()

    @pl.loop(1, n)
    def _(d):
        pl.semaphore_signal(barrier, inc=1, device_id={"smp": lax.rem(me + d, n)})

    @pl.when(has_next)
    def _():
        pl.semaphore_signal(barrier, inc=1, device_id={"snp": core + 1})

    @pl.when(has_prev)
    def _():
        pl.semaphore_signal(barrier, inc=1, device_id={"snp": core - 1})

    load = pltpu.make_async_copy(x_ref, full.at[pl.ds(0, samples), pl.ds(0, cols)], local_sem)
    load.start()
    pl.semaphore_wait(barrier, n - 1 + jnp.where(has_next, 1, 0) + jnp.where(has_prev, 1, 0))

    def raw(b):
        return pltpu.make_async_remote_copy(
            x_ref.at[:, pl.ds(b * BLK, BLK)],
            full.at[pl.ds(samples, samples), pl.ds(b * BLK, BLK)],
            raw_ss.at[b], raw_rs.at[b], device_id={"smp": near_peer})

    def to_core():
        return pltpu.make_async_remote_copy(
            x_ref.at[:, pl.ds(0, 2 * BLK)],
            full.at[pl.ds(0, samples), pl.ds(cols, 2 * BLK)],
            core_ss, core_rs, device_id={"snp": lax.rem(core + snps - 1, snps)})

    def forward(b):
        return pltpu.make_async_remote_copy(
            full.at[pl.ds(samples, samples), pl.ds(pl.multiple_of(b * BLK, BLK), BLK)],
            full.at[pl.ds(samples, samples), pl.ds(pl.multiple_of(cols + b * BLK, BLK), BLK)],
            fwd_ss.at[b], fwd_rs.at[b], device_id={"snp": lax.rem(core + snps - 1, snps)})

    for b in range(blocks):
        raw(b).start()

    @pl.when(has_prev)
    def _():
        to_core().start()

    load.wait()
    for b in range(blocks):
        def add(r, total, b=b):
            piece = full[pl.ds(pl.multiple_of(r * 16, 16), 16), b * BLK:(b + 1) * BLK].astype(jnp.float32)
            return total + piece * piece
        total = lax.fori_loop(0, samples // 16, add, jnp.zeros((16, BLK), jnp.float32))
        squares_all[me, :, b * BLK:(b + 1) * BLK] = jnp.sum(total, axis=0, keepdims=True)

    def send_squares(d):
        peer = lax.rem(me + d, n)
        return pltpu.make_async_remote_copy(
            squares_all.at[me], squares_all.at[me], sq_ss.at[peer], sq_rs.at[me], device_id={"smp": peer})

    def recv_squares(d):
        peer = lax.rem(me + d, n)
        return pltpu.make_async_remote_copy(
            squares_all.at[peer], squares_all.at[peer], sq_ss.at[peer], sq_rs.at[peer], device_id={"smp": peer})

    @pl.loop(1, n)
    def _(d):
        send_squares(d).start()

    @pl.loop(1, n)
    def _(d):
        recv_squares(d).wait_recv()

    squares = lax.fori_loop(0, n, lambda i, s: s + squares_all[i], jnp.zeros((1, cols), jnp.float32))
    next_squares[0] = squares[:, : 2 * BLK]

    def to_core_squares():
        return pltpu.make_async_remote_copy(
            next_squares.at[0], next_squares.at[1], nsq_ss, nsq_rs,
            device_id={"snp": lax.rem(core + snps - 1, snps)})

    @pl.when(has_prev)
    def _():
        to_core_squares().start()

    own_scale = lax.rsqrt(squares + EPS)
    for b in range(blocks):
        scale[b] = own_scale[:, b * BLK:(b + 1) * BLK]
        for f in range(2):
            lanes = [own_scale[:, b * BLK + q * quarter:b * BLK + (q + 1) * quarter] for q in (2 * f, 2 * f + 1)]
            line = jnp.where(near == 0, lanes[0], lanes[1]) * UNIT
            row_scale[b, f * quarter:(f + 1) * quarter] = jnp.transpose(
                jnp.broadcast_to(line, (quarter, quarter)))

    @pl.when(has_next)
    def _():
        to_core_squares().wait_recv()
        nxt = lax.rsqrt(next_squares[1] + EPS)
        scale[blocks] = nxt[:, :BLK]
        scale[blocks + 1] = nxt[:, BLK:]
        to_core().wait_recv()

    def where(i):
        m, k = i // 3, i % 3
        b = m - k
        there = (b >= 0) & (b < blocks) & ((m < blocks) | has_next)
        return m, k, b, there

    def slot(k, b):
        return k * blocks + b

    def level_copy(level, t):
        v = (me // bits[level]) % 2
        return pltpu.make_async_remote_copy(
            level_send[level].at[t], level_recv[level].at[t], lev_ss.at[level, t], lev_rs.at[level, t],
            device_id={"smp": me + bits[level] * (1 - 2 * v)})

    def far_copy(t):
        return pltpu.make_async_remote_copy(
            far_send.at[t], far_recv.at[t], far_ss.at[t], far_rs.at[t], device_id={"smp": far_peer})

    def row0(level):
        lo = 0
        for j in range(level):
            lo = lo + ((me // bits[j]) % 2) * (quarter >> (j + 1))
        return lo

    def part(level):
        rows = quarter >> level
        return pl.ds(pl.multiple_of(row0(level), rows), rows)

    def send_level(level, t):
        rows = quarter >> (level + 1)
        v = (me // bits[level]) % 2
        start = pl.multiple_of(row0(level) + (1 - v) * rows, rows)
        level_send[level][t] = acc[t, :, pl.ds(start, rows), :].astype(WIRE)
        level_copy(level, t).start()

    def send_next(level, t):
        if level < len(bits):
            send_level(level, t)
        else:
            far_send[t] = acc[t, 1 - far, part(level), :].astype(WIRE)
            far_copy(t).start()

    def step(i):
        m, k, b, there = where(i)
        inside = i < 3 * (blocks + 2)

        @pl.when(inside & (k == 0))
        def _():
            @pl.when(m < blocks)
            def _():
                raw(pl.multiple_of(m, 1)).wait_recv()

                @pl.when(has_prev & (m < 2))
                def _():
                    forward(m).start()

            @pl.when((m >= blocks) & has_next)
            def _():
                forward(m - blocks).wait_recv()

        @pl.when(inside & there)
        def _():
            t = slot(k, b)
            lhs = jnp.concatenate(
                [full[:, pl.ds(pl.multiple_of(b * BLK + (near + 2 * f) * quarter, quarter), quarter)]
                 for f in range(2)], axis=1)
            rhs = full[:, pl.ds(pl.multiple_of(m * BLK, BLK), BLK)]
            gram = lax.dot_general(lhs, rhs, (((0,), (0,)), ((), ())), preferred_element_type=jnp.float32)
            rs = row_scale[b]
            gram = gram * jnp.concatenate([rs] * (BLK // quarter), axis=1) * scale[m]
            acc[t] = gram.reshape(2, quarter, BLK)
            send_next(0, t)

        @pl.when(inside & (b >= 0) & (b < blocks) & jnp.logical_not(there))
        def _():
            out_ref[k, b] = jnp.zeros(out_ref.shape[2:], jnp.float32)

        for level in range(len(bits)):
            j = i - LAG * (level + 1)
            _, k2, b2, there2 = where(jnp.maximum(j, 0))

            @pl.when((j >= 0) & (j < 3 * (blocks + 2)) & there2)
            def _(level=level, k2=k2, b2=b2):
                t = slot(k2, b2)
                level_copy(level, t).wait_recv()
                mine = part(level + 1)
                acc[t, :, mine, :] = acc[t, :, mine, :] + level_recv[level][t].astype(jnp.float32)
                send_next(level + 1, t)

        j = i - LAG * (len(bits) + 1)
        _, k3, b3, there3 = where(jnp.maximum(j, 0))

        @pl.when((j >= 0) & there3)
        def _():
            t = slot(k3, b3)
            far_copy(t).wait_recv()
            total = acc[t, far, part(len(bits)), :] + far_recv[t].astype(jnp.float32)
            out_ref[k3, b3] = total * (1.0 / UNIT)

    @pl.loop(0, 3 * (blocks + 2) + LAG * (len(bits) + 1))
    def _(i):
        step(i)

    @pl.loop(1, n)
    def _(d):
        send_squares(d).wait_send()

    for b in range(blocks):
        raw(b).wait_send()

    @pl.when(has_prev)
    def _():
        to_core().wait_send()
        to_core_squares().wait_send()
        forward(0).wait_send()
        forward(1).wait_send()

    @pl.loop(0, 3 * (blocks + 2))
    def _(i):
        _, k, b, there = where(i)

        @pl.when(there)
        def _():
            t = slot(k, b)
            for level in range(len(bits)):
                level_copy(level, t).wait_send()
            far_copy(t).wait_send()


def shards(n, snps, dosage):
    samples, cols = dosage.shape
    blocks = cols // BLK
    tiles = 3 * blocks
    rows = BLK // n
    quarter = BLK // 4
    levels = max(0, (n // 4).bit_length() - 1)
    vmem = pltpu.VMEM
    sizes = [(tiles, 2, quarter >> (j + 1), BLK) for j in range(levels)]
    dma = pltpu.SemaphoreType.DMA
    scratch = [
        vmem((2 * samples, cols + 2 * BLK), jnp.bfloat16),
        vmem((n, 1, cols), jnp.float32),
        vmem((blocks + 2, 1, BLK), jnp.float32),
        vmem((blocks, 2 * quarter, quarter), jnp.float32),
        vmem((tiles, 2, quarter, BLK), jnp.float32),
        [vmem(s, WIRE) for s in sizes],
        [vmem(s, WIRE) for s in sizes],
        vmem((tiles, rows, BLK), WIRE),
        vmem((tiles, rows, BLK), WIRE),
        vmem((2, 1, 2 * BLK), jnp.float32),
        dma, dma((blocks,)), dma((blocks,)), dma, dma, dma((2,)), dma((2,)),
        dma((n,)), dma((n,)), dma, dma,
        dma((levels, tiles)), dma((levels, tiles)), dma((tiles,)), dma((tiles,)),
    ]
    flops = 2 * tiles * BLK * BLK * samples
    return pl.pallas_call(
        functools.partial(kernel, n, snps),
        out_shape=jax.ShapeDtypeStruct((3, blocks, rows, BLK), jnp.float32),
        in_specs=[pl.BlockSpec(memory_space=pl.ANY)],
        out_specs=pl.BlockSpec(memory_space=pltpu.VMEM),
        scratch_shapes=scratch,
        compiler_params=pltpu.CompilerParams(
            collective_id=0, has_side_effects=True, vmem_limit_bytes=48 * 2**20),
        cost_estimate=pl.CostEstimate(flops=flops, bytes_accessed=4 * samples * cols, transcendentals=0),
    )(dosage)


def solution(mesh):
    return jax.shard_map(
        functools.partial(shards, mesh.shape["smp"], mesh.shape["snp"]),
        mesh=mesh,
        in_specs=(P("smp", ("seg", "snp")),),
        out_specs=P(None, ("seg", "snp"), "smp", None),
        check_vma=False,
    )
```

time: 462 us -> 126 us (0.27)
  waiting for transfers between devices: 360 us -> 0 us
  Pallas kernels: 0 us -> 124 us
  blocking collectives: 41 us -> 0 us
  local copies, waits for them, and re-layouts: 29.3 us -> 2.74 us
  between operations: 14.1 us -> 0.01 us
  matrix products: 10.3 us -> 0 us
  other arithmetic: 5.45 us -> 0 us
    unnamed x2 -> x0, waiting for transfers between devices: 360 us -> none
    pallas_call x0 -> x1, Pallas kernels: none -> 124 us  [shards(): pl.pallas_call(functools.partial(kernel, n, snps), out_shape=jax.ShapeDty...]
    psum x1 -> x0, blocking collectives: 41 us -> none  [shards(): square_sums = lax.psum(squares, 'smp').reshape(block_count + 2, BLK)]
    another operation x5 -> x0, local copies, waits for them, and re-layouts: 15.7 us -> none  [the longest x2 15.7 us: make_tiles(): return jnp.stack(tile_list, axis=1)]
    dot_general x3 -> x0, matrix products: 10.3 us -> none  [make_tiles(): jnp.einsum('hmn,hmq->nmq', own_cube, right_cube[:, offset:offset + block_...]
  transfers between devices with their start and end apart: 2 -> 0, of which waited for: 1 -> 0; matrix products, arithmetic and copies ran while one was open for 3% -> 0% of each run, Pallas kernels for 0% -> 0%
where the time goes in v1:
time: 126 us
  Pallas kernels  124 us (98%)
  local copies, waits for them, and re-layouts  2.74 us (2%)
    pallas_call x1, Pallas kernels, shards(): pl.pallas_call(functools.partial(kernel, n, snps), out_shape=jax.ShapeDty...  124 us
    unnamed x3, local copies, waits for them, and re-layouts  2.74 us

profile of v1, /device:TPU:0, one launch (start us, length us, event | category | flops | bytes accessed | tf_op | source)
XLA Modules:
  0.0 126.3 jit_solution(13525923294508696011)
XLA Ops:
  0.0 0.0 copy-start
  0.0 1.6 %copy-done = bf16[512,2048]{1,0:T(8,128)(2,1)S(1)} copy-done((bf16[512,2048]{1,0:T(8,128)(2,1)S(1)}, bf16[512,2048]{1,0:T(8,128)(2,1)}, u32[]{:S(2)}) %copy-start) | copy-done | bytes 2097176
  1.6 123.6 %shard_map.17 = f32[3,4,64,512]{3,2,1,0:T(8,128)S(1)} custom-call(bf16[512,2048]{1,0:T(8,128)(2,1)S(1)} %copy-done), custom_call_target="tpu_custom_call" | custom-call | flops 3221225472 | bytes 4194304 | tf_op jit(solution)/shard_map/pallas_call | solution.py:293
  125.2 1.1 copy.3
Async XLA Ops:
  0.0 1.6 %copy-start = (bf16[512,2048]{1,0:T(8,128)(2,1)S(1)}, bf16[512,2048]{1,0:T(8,128)(2,1)}, u32[]{:S(2)}) copy-start(bf16[512,2048]{1,0:T(8,128)(2,1)} %x_ref.1) | copy-start | bytes 6291460

commit v2 on v1

--- a/solution.py
+++ b/solution.py
@@ -9,9 +9,22 @@
 
 BLK = 512
 EPS = 1e-06
-WIRE = jnp.float32
-UNIT = 1.0
+WIRE = jnp.bfloat16
+UNIT = 256.0
 LAG = 3
+
+
+def pack(v):
+    v2 = v * v
+    v4 = v2 * v2
+    return (v * v2 * v4 * (v4 * v4)).astype(WIRE)
+
+
+def unpack(y):
+    y = y.astype(jnp.float32)
+    size = jnp.abs(y)
+    root = jnp.exp2(jnp.log2(jnp.maximum(size, 2.0**-126)) * (1.0 / 15.0))
+    return jnp.where(size < 2.0**-126, 0.0, jnp.where(y < 0, -root, root))
 
 
 def kernel(n, snps, x_ref, out_ref, full, squares_all, scale, row_scale, acc, level_send, level_recv,
@@ -72,8 +85,7 @@
             full.at[pl.ds(samples, samples), pl.ds(pl.multiple_of(cols + b * BLK, BLK), BLK)],
             fwd_ss.at[b], fwd_rs.at[b], device_id={"snp": lax.rem(core + snps - 1, snps)})
 
-    for b in range(blocks):
-        raw(b).start()
+    raw(0).start()
 
     @pl.when(has_prev)
     def _():
@@ -167,14 +179,15 @@
         rows = quarter >> (level + 1)
         v = (me // bits[level]) % 2
         start = pl.multiple_of(row0(level) + (1 - v) * rows, rows)
-        level_send[level][t] = acc[t, :, pl.ds(start, rows), :].astype(WIRE)
+        level_send[level][t] = pack(acc[t, :, pl.ds(start, rows), :].reshape(2 * rows, BLK))
         level_copy(level, t).start()
 
     def send_next(level, t):
         if level < len(bits):
             send_level(level, t)
         else:
-            far_send[t] = acc[t, 1 - far, part(level), :].astype(WIRE)
+            theirs = acc[t, 1 - far, part(level), :]
+            far_send[t] = pack(jnp.concatenate([theirs[:, :BLK // 2], theirs[:, BLK // 2:]], axis=0))
             far_copy(t).start()
 
     def step(i):
@@ -185,7 +198,11 @@
         def _():
             @pl.when(m < blocks)
             def _():
-                raw(pl.multiple_of(m, 1)).wait_recv()
+                raw(m).wait_recv()
+
+                @pl.when(m + 1 < blocks)
+                def _():
+                    raw(m + 1).start()
 
                 @pl.when(has_prev & (m < 2))
                 def _():
@@ -221,7 +238,8 @@
                 t = slot(k2, b2)
                 level_copy(level, t).wait_recv()
                 mine = part(level + 1)
-                acc[t, :, mine, :] = acc[t, :, mine, :] + level_recv[level][t].astype(jnp.float32)
+                other = unpack(level_recv[level][t]).reshape(2, quarter >> (level + 1), BLK)
+                acc[t, :, mine, :] = acc[t, :, mine, :] + other
                 send_next(level + 1, t)
 
         j = i - LAG * (len(bits) + 1)
@@ -231,7 +249,10 @@
         def _():
             t = slot(k3, b3)
             far_copy(t).wait_recv()
-            total = acc[t, far, part(len(bits)), :] + far_recv[t].astype(jnp.float32)
+            other = unpack(far_recv[t])
+            rows = BLK // n
+            other = jnp.concatenate([other[:rows], other[rows:]], axis=1)
+            total = acc[t, far, part(len(bits)), :] + other
             out_ref[k3, b3] = total * (1.0 / UNIT)
 
     @pl.loop(0, 3 * (blocks + 2) + LAG * (len(bits) + 1))
@@ -272,7 +293,7 @@
     quarter = BLK // 4
     levels = max(0, (n // 4).bit_length() - 1)
     vmem = pltpu.VMEM
-    sizes = [(tiles, 2, quarter >> (j + 1), BLK) for j in range(levels)]
+    sizes = [(tiles, quarter >> j, BLK) for j in range(levels)]
     dma = pltpu.SemaphoreType.DMA
     scratch = [
         vmem((2 * samples, cols + 2 * BLK), jnp.bfloat16),
@@ -282,8 +303,8 @@
         vmem((tiles, 2, quarter, BLK), jnp.float32),
         [vmem(s, WIRE) for s in sizes],
         [vmem(s, WIRE) for s in sizes],
-        vmem((tiles, rows, BLK), WIRE),
-        vmem((tiles, rows, BLK), WIRE),
+        vmem((tiles, 2 * rows, BLK // 2), WIRE),
+        vmem((tiles, 2 * rows, BLK // 2), WIRE),
         vmem((2, 1, 2 * BLK), jnp.float32),
         dma, dma((blocks,)), dma((blocks,)), dma, dma, dma((2,)), dma((2,)),
         dma((n,)), dma((n,)), dma, dma,

time: 126 us -> 85.6 us (0.68)
  Pallas kernels: 124 us -> 82.7 us
    pallas_call x1, Pallas kernels: 124 us -> 82.7 us  [shards(): pl.pallas_call(functools.partial(kernel, n, snps), out_shape=jax.ShapeDty...]
where the time goes in v2:
time: 85.6 us; the launch traced here: 85.5 us
  Pallas kernels  82.7 us (97%)
  local copies, waits for them, and re-layouts  2.74 us (3%)
    pallas_call x1, Pallas kernels, shards(): pl.pallas_call(functools.partial(kernel, n, snps), out_shape=jax.ShapeDty...  82.7 us
    unnamed x3, local copies, waits for them, and re-layouts  2.74 us

profile of v2, /device:TPU:0, one launch (start us, length us, event | category | flops | bytes accessed | tf_op | source)
XLA Modules:
  0.0 85.5 jit_solution(15884460096143426804)
XLA Ops:
  0.0 0.0 copy-start
  0.0 1.6 %copy-done = bf16[512,2048]{1,0:T(8,128)(2,1)S(1)} copy-done((bf16[512,2048]{1,0:T(8,128)(2,1)S(1)}, bf16[512,2048]{1,0:T(8,128)(2,1)}, u32[]{:S(2)}) %copy-start) | copy-done | bytes 2097176
  1.6 82.7 %shard_map.17 = f32[3,4,64,512]{3,2,1,0:T(8,128)S(1)} custom-call(bf16[512,2048]{1,0:T(8,128)(2,1)S(1)} %copy-done), custom_call_target="tpu_custom_call" | custom-call | flops 3221225472 | bytes 4194304 | tf_op jit(solution)/shard_map/pallas_call | solution.py:314
  84.3 1.1 %copy.3 = f32[3,4,64,512]{3,2,1,0:T(8,128)} copy(f32[3,4,64,512]{3,2,1,0:T(8,128)S(1)} %shard_map.17) | data formatting | bytes 3145728
Async XLA Ops:
  0.0 1.6 %copy-start = (bf16[512,2048]{1,0:T(8,128)(2,1)S(1)}, bf16[512,2048]{1,0:T(8,128)(2,1)}, u32[]{:S(2)}) copy-start(bf16[512,2048]{1,0:T(8,128)(2,1)} %x_ref.1) | copy-start | bytes 6291460

commit v3 on v2

--- a/solution.py
+++ b/solution.py
@@ -67,11 +67,18 @@
     load.start()
     pl.semaphore_wait(barrier, n - 1 + jnp.where(has_next, 1, 0) + jnp.where(has_prev, 1, 0))
 
-    def raw(b):
-        return pltpu.make_async_remote_copy(
-            x_ref.at[:, pl.ds(b * BLK, BLK)],
-            full.at[pl.ds(samples, samples), pl.ds(b * BLK, BLK)],
-            raw_ss.at[b], raw_rs.at[b], device_id={"smp": near_peer})
+    def arrival(m):
+        return jnp.where(has_next, blocks - 1 - m, m)
+
+    half = samples // 2
+
+    def raw(j):
+        b = pl.multiple_of(arrival(j // 2) * BLK, BLK)
+        r = pl.multiple_of((j % 2) * half, half)
+        return pltpu.make_async_remote_copy(
+            x_ref.at[pl.ds(r, half), pl.ds(b, BLK)],
+            full.at[pl.ds(pl.multiple_of(samples + r, half), half), pl.ds(b, BLK)],
+            raw_ss.at[j], raw_rs.at[j], device_id={"smp": near_peer})
 
     def to_core():
         return pltpu.make_async_remote_copy(
@@ -86,6 +93,7 @@
             fwd_ss.at[b], fwd_rs.at[b], device_id={"snp": lax.rem(core + snps - 1, snps)})
 
     raw(0).start()
+    raw(1).start()
 
     @pl.when(has_prev)
     def _():
@@ -146,11 +154,16 @@
         scale[blocks + 1] = nxt[:, BLK:]
         to_core().wait_recv()
 
+    @pl.when(jnp.logical_not(has_next))
+    def _():
+        for k in range(1, 3):
+            for b in range(blocks - k, blocks):
+                out_ref[k, b] = jnp.zeros(out_ref.shape[2:], jnp.float32)
+
     def where(i):
         m, k = i // 3, i % 3
-        b = m - k
-        there = (b >= 0) & (b < blocks) & ((m < blocks) | has_next)
-        return m, k, b, there
+        b = jnp.where(has_next, blocks - 1 - m, m - k)
+        return m, k, b, b >= 0
 
     def slot(k, b):
         return k * blocks + b
@@ -192,25 +205,24 @@
 
     def step(i):
         m, k, b, there = where(i)
-        inside = i < 3 * (blocks + 2)
+        inside = i < tiles
 
         @pl.when(inside & (k == 0))
         def _():
-            @pl.when(m < blocks)
-            def _():
-                raw(m).wait_recv()
+            for h in range(2):
+                raw(2 * m + h).wait_recv()
 
                 @pl.when(m + 1 < blocks)
                 def _():
-                    raw(m + 1).start()
-
-                @pl.when(has_prev & (m < 2))
-                def _():
-                    forward(m).start()
-
-            @pl.when((m >= blocks) & has_next)
+                    raw(2 * m + 2 + h).start()
+
+            @pl.when(has_prev & (arrival(m) < 2))
             def _():
-                forward(m - blocks).wait_recv()
+                forward(arrival(m)).start()
+
+        @pl.when(has_next & (m == 0) & (k >= 1))
+        def _():
+            forward(k - 1).wait_recv()
 
         @pl.when(inside & there)
         def _():
@@ -218,22 +230,18 @@
             lhs = jnp.concatenate(
                 [full[:, pl.ds(pl.multiple_of(b * BLK + (near + 2 * f) * quarter, quarter), quarter)]
                  for f in range(2)], axis=1)
-            rhs = full[:, pl.ds(pl.multiple_of(m * BLK, BLK), BLK)]
+            rhs = full[:, pl.ds(pl.multiple_of((b + k) * BLK, BLK), BLK)]
             gram = lax.dot_general(lhs, rhs, (((0,), (0,)), ((), ())), preferred_element_type=jnp.float32)
             rs = row_scale[b]
-            gram = gram * jnp.concatenate([rs] * (BLK // quarter), axis=1) * scale[m]
+            gram = gram * jnp.concatenate([rs] * (BLK // quarter), axis=1) * scale[b + k]
             acc[t] = gram.reshape(2, quarter, BLK)
             send_next(0, t)
-
-        @pl.when(inside & (b >= 0) & (b < blocks) & jnp.logical_not(there))
-        def _():
-            out_ref[k, b] = jnp.zeros(out_ref.shape[2:], jnp.float32)
 
         for level in range(len(bits)):
             j = i - LAG * (level + 1)
             _, k2, b2, there2 = where(jnp.maximum(j, 0))
 
-            @pl.when((j >= 0) & (j < 3 * (blocks + 2)) & there2)
+            @pl.when((j >= 0) & (j < tiles) & there2)
             def _(level=level, k2=k2, b2=b2):
                 t = slot(k2, b2)
                 level_copy(level, t).wait_recv()
@@ -255,7 +263,7 @@
             total = acc[t, far, part(len(bits)), :] + other
             out_ref[k3, b3] = total * (1.0 / UNIT)
 
-    @pl.loop(0, 3 * (blocks + 2) + LAG * (len(bits) + 1))
+    @pl.loop(0, tiles + LAG * (len(bits) + 1))
     def _(i):
         step(i)
 
@@ -263,8 +271,8 @@
     def _(d):
         send_squares(d).wait_send()
 
-    for b in range(blocks):
-        raw(b).wait_send()
+    for j in range(2 * blocks):
+        raw(j).wait_send()
 
     @pl.when(has_prev)
     def _():
@@ -273,7 +281,7 @@
         forward(0).wait_send()
         forward(1).wait_send()
 
-    @pl.loop(0, 3 * (blocks + 2))
+    @pl.loop(0, tiles)
     def _(i):
         _, k, b, there = where(i)
 
@@ -306,7 +314,7 @@
         vmem((tiles, 2 * rows, BLK // 2), WIRE),
         vmem((tiles, 2 * rows, BLK // 2), WIRE),
         vmem((2, 1, 2 * BLK), jnp.float32),
-        dma, dma((blocks,)), dma((blocks,)), dma, dma, dma((2,)), dma((2,)),
+        dma, dma((2 * blocks,)), dma((2 * blocks,)), dma, dma, dma((2,)), dma((2,)),
         dma((n,)), dma((n,)), dma, dma,
         dma((levels, tiles)), dma((levels, tiles)), dma((tiles,)), dma((tiles,)),
     ]

time: 85.6 us -> 81 us (0.946)
  Pallas kernels: 82.7 us -> 78.1 us
    pallas_call x1, Pallas kernels: 82.7 us -> 78.1 us  [shards(): pl.pallas_call(functools.partial(kernel, n, snps), out_shape=jax.ShapeDty...]
where the time goes in v3:
time: 81 us; the launch traced here: 80.9 us
  Pallas kernels  78.1 us (96%)
  local copies, waits for them, and re-layouts  2.74 us (3%)
    pallas_call x1, Pallas kernels, shards(): pl.pallas_call(functools.partial(kernel, n, snps), out_shape=jax.ShapeDty...  78.1 us
    unnamed x3, local copies, waits for them, and re-layouts  2.74 us

profile of v3, /device:TPU:0, one launch (start us, length us, event | category | flops | bytes accessed | tf_op | source)
XLA Modules:
  0.0 80.9 jit_solution(5807424151806763555)
XLA Ops:
  0.0 0.0 copy-start
  0.0 1.6 %copy-done = bf16[512,2048]{1,0:T(8,128)(2,1)S(1)} copy-done((bf16[512,2048]{1,0:T(8,128)(2,1)S(1)}, bf16[512,2048]{1,0:T(8,128)(2,1)}, u32[]{:S(2)}) %copy-start) | copy-done | bytes 2097176
  1.6 78.1 %shard_map.17 = f32[3,4,64,512]{3,2,1,0:T(8,128)S(1)} custom-call(bf16[512,2048]{1,0:T(8,128)(2,1)S(1)} %copy-done), custom_call_target="tpu_custom_call" | custom-call | flops 3221225472 | bytes 4194304 | tf_op jit(solution)/shard_map/pallas_call | solution.py:322
  79.7 1.1 %copy.3 = f32[3,4,64,512]{3,2,1,0:T(8,128)} copy(f32[3,4,64,512]{3,2,1,0:T(8,128)S(1)} %shard_map.17) | data formatting | bytes 3145728
Async XLA Ops:
  0.0 1.6 %copy-start = (bf16[512,2048]{1,0:T(8,128)(2,1)S(1)}, bf16[512,2048]{1,0:T(8,128)(2,1)}, u32[]{:S(2)}) copy-start(bf16[512,2048]{1,0:T(8,128)(2,1)} %x_ref.1) | copy-start | bytes 6291460

commit v4 on v3

--- a/solution.py
+++ b/solution.py
@@ -11,7 +11,8 @@
 EPS = 1e-06
 WIRE = jnp.bfloat16
 UNIT = 256.0
-LAG = 3
+LAG = 2
+FAR_LAG = 3
 
 
 def pack(v):
@@ -250,7 +251,7 @@
                 acc[t, :, mine, :] = acc[t, :, mine, :] + other
                 send_next(level + 1, t)
 
-        j = i - LAG * (len(bits) + 1)
+        j = i - (LAG * len(bits) + FAR_LAG)
         _, k3, b3, there3 = where(jnp.maximum(j, 0))
 
         @pl.when((j >= 0) & there3)
@@ -263,7 +264,7 @@
             total = acc[t, far, part(len(bits)), :] + other
             out_ref[k3, b3] = total * (1.0 / UNIT)
 
-    @pl.loop(0, tiles + LAG * (len(bits) + 1))
+    @pl.loop(0, tiles + (LAG * len(bits) + FAR_LAG))
     def _(i):
         step(i)
 

time: 81 us -> 79.6 us (0.983)
  Pallas kernels: 78.1 us -> 76.7 us
    pallas_call x1, Pallas kernels: 78.1 us -> 76.7 us  [shards(): pl.pallas_call(functools.partial(kernel, n, snps), out_shape=jax.ShapeDty...]
where the time goes in v4:
time: 79.6 us; the launch traced here: 79.5 us
  Pallas kernels  76.7 us (96%)
  local copies, waits for them, and re-layouts  2.74 us (3%)
    pallas_call x1, Pallas kernels, shards(): pl.pallas_call(functools.partial(kernel, n, snps), out_shape=jax.ShapeDty...  76.7 us
    unnamed x3, local copies, waits for them, and re-layouts  2.74 us

profile of v4, /device:TPU:0, one launch (start us, length us, event | category | flops | bytes accessed | tf_op | source)
XLA Modules:
  0.0 79.5 jit_solution(11208089806353645293)
XLA Ops:
  0.0 0.0 copy-start
  0.0 1.6 %copy-done = bf16[512,2048]{1,0:T(8,128)(2,1)S(1)} copy-done((bf16[512,2048]{1,0:T(8,128)(2,1)S(1)}, bf16[512,2048]{1,0:T(8,128)(2,1)}, u32[]{:S(2)}) %copy-start) | copy-done | bytes 2097176
  1.6 76.7 %shard_map.17 = f32[3,4,64,512]{3,2,1,0:T(8,128)S(1)} custom-call(bf16[512,2048]{1,0:T(8,128)(2,1)S(1)} %copy-done), custom_call_target="tpu_custom_call" | custom-call | flops 3221225472 | bytes 4194304 | tf_op jit(solution)/shard_map/pallas_call | solution.py:323
  78.3 1.1 %copy.3 = f32[3,4,64,512]{3,2,1,0:T(8,128)} copy(f32[3,4,64,512]{3,2,1,0:T(8,128)S(1)} %shard_map.17) | data formatting | bytes 3145728
Async XLA Ops:
  0.0 1.6 %copy-start = (bf16[512,2048]{1,0:T(8,128)(2,1)S(1)}, bf16[512,2048]{1,0:T(8,128)(2,1)}, u32[]{:S(2)}) copy-start(bf16[512,2048]{1,0:T(8,128)(2,1)} %x_ref.1) | copy-start | bytes 6291460

commit v5 on v4

--- a/solution.py
+++ b/solution.py
@@ -95,6 +95,7 @@
 
     raw(0).start()
     raw(1).start()
+    raw(2).start()
 
     @pl.when(has_prev)
     def _():
@@ -213,9 +214,9 @@
             for h in range(2):
                 raw(2 * m + h).wait_recv()
 
-                @pl.when(m + 1 < blocks)
+                @pl.when(2 * m + h + 3 < 2 * blocks)
                 def _():
-                    raw(2 * m + 2 + h).start()
+                    raw(2 * m + h + 3).start()
 
             @pl.when(has_prev & (arrival(m) < 2))
             def _():

time: 79.6 us -> 80.3 us (level)
  no operation moved by 1% of the time
where the time goes in v5:
time: 80.3 us; the launch traced here: 80.2 us
  Pallas kernels  77.5 us (97%)
  local copies, waits for them, and re-layouts  2.74 us (3%)
    pallas_call x1, Pallas kernels, shards(): pl.pallas_call(functools.partial(kernel, n, snps), out_shape=jax.ShapeDty...  77.5 us
    unnamed x3, local copies, waits for them, and re-layouts  2.74 us

profile of v5, /device:TPU:0, one launch (start us, length us, event | category | flops | bytes accessed | tf_op | source)
XLA Modules:
  0.0 80.2 jit_solution(18162445658178530727)
XLA Ops:
  0.0 0.0 copy-start
  0.0 1.6 %copy-done = bf16[512,2048]{1,0:T(8,128)(2,1)S(1)} copy-done((bf16[512,2048]{1,0:T(8,128)(2,1)S(1)}, bf16[512,2048]{1,0:T(8,128)(2,1)}, u32[]{:S(2)}) %copy-start) | copy-done | bytes 2097176
  1.6 77.5 %shard_map.17 = f32[3,4,64,512]{3,2,1,0:T(8,128)S(1)} custom-call(bf16[512,2048]{1,0:T(8,128)(2,1)S(1)} %copy-done), custom_call_target="tpu_custom_call" | custom-call | flops 3221225472 | bytes 4194304 | tf_op jit(solution)/shard_map/pallas_call | solution.py:324
  79.1 1.1 %copy.3 = f32[3,4,64,512]{3,2,1,0:T(8,128)} copy(f32[3,4,64,512]{3,2,1,0:T(8,128)S(1)} %shard_map.17) | data formatting | bytes 3145728
Async XLA Ops:
  0.0 1.6 %copy-start = (bf16[512,2048]{1,0:T(8,128)(2,1)S(1)}, bf16[512,2048]{1,0:T(8,128)(2,1)}, u32[]{:S(2)}) copy-start(bf16[512,2048]{1,0:T(8,128)(2,1)} %x_ref.1) | copy-start | bytes 6291460
